TPU v7x, 32 devices: a whole 2x2x4 slice. The times are simulated.
32 devices in a mesh: dp: 4 (over y, x), tensor: 8 (over z, core).
Axes of the slice: x: 2, y: 2, z: 4, core: 2. Of those that a mesh axis runs over, the one named last changes fastest.
Arguments:
- inputs: bfloat16 [512, 4096], P('dp', 'tensor'), may hold values from -6 to 6
- cotangent: bfloat16 [512, 4096], P('dp', 'tensor'), may hold values from -6 to 6
- gate_w: bfloat16 [8, 96, 128, 128], P('tensor'), may hold values from -0.25 to 0.25
- up_w: bfloat16 [8, 96, 128, 128], P('tensor'), may hold values from -0.25 to 0.25
- down_w: bfloat16 [8, 96, 128, 128], P('tensor'), may hold values from -0.25 to 0.25
- gate_list: int32 [8, 96], P('tensor'), may hold values from -1 to 511, as said below
- up_list: int32 [8, 96], P('tensor'), may hold values from -1 to 511, as said below
- down_list: int32 [8, 96], P('tensor'), may hold values from -1 to 511, as said below
Outputs:
- grad_x: bfloat16 [512, 4096], P('dp', 'tensor')
- grad_gate_w: bfloat16 [8, 96, 128, 128], P('tensor', None, 'dp')
- grad_up_w: bfloat16 [8, 96, 128, 128], P('tensor', None, 'dp')
- grad_down_w: bfloat16 [8, 96, 128, 128], P('tensor', None, 'dp')
Inputs may be any that keep to these rules, and one draw needn't show every extreme that they name: `gate_list`: row j of the list names blocks of hidden blocks j * 16 to j * 16 + 15 only; no entry appears twice in a row; live entries come first and -1 fills the rest; a row holds at most 96 live entries and some row holds exactly 96. `up_list`: as for gate_list, drawn independently. `down_list`: as for gate_list, drawn independently.
All inputs are finite; a program needn't handle non-finite values.
Results may differ from a plain program's by a relative error of at most 0.014.
Values may be sent and summed in bfloat16 or wider, within the bound.
A program may use at most 128 MiB of HBM per device.

v0:
```python
import functools
import math

import jax
import jax.numpy as jnp
from jax import lax
from jax.experimental import pallas as pl
from jax.experimental.pallas import tpu as pltpu
from jax.sharding import PartitionSpec as P

D = 4096
FF = 16384
BLOCK = 128
UNROLL = 2
BACK_UNROLL = 4
SLOT_UNROLL = 8
F32 = jnp.float32
BF16 = jnp.bfloat16


def decode(entries, row_count):
    living = entries >= 0
    clamped = jnp.maximum(entries, 0)
    return (living, clamped // row_count, clamped % row_count)


def one_hot(block_index, width_count, living):
    return ((block_index[:, None] == jnp.arange(width_count)[None, :]) & living[:, None]).astype(
        jnp.float32
    )


def select_sum(values, table):
    return jnp.sum(values[:, :, None, :] * table[None, :, :, None], axis=1)


def project_rows(blocks_in, weights, rows_hot):
    products = jnp.einsum("tkc,kch->tkh", blocks_in, weights, preferred_element_type=jnp.float32)
    return select_sum(products, rows_hot)


def weight_term(products, grad_scale, living):
    rounded = (products * grad_scale).astype(jnp.bfloat16)
    rounded = lax.optimization_barrier(rounded)
    return (rounded.astype(jnp.float32) * living[:, None, None].astype(jnp.float32))[None]


def add_sources(received):
    return jnp.sum(received.astype(jnp.float32), axis=1)


def plain_on_device(inputs, cotangent, gate_w, up_w, down_w, gate_list, up_list, down_list):
    tensor_size = lax.axis_size("tensor")
    hidden_rows = FF // (BLOCK * tensor_size)
    feat_blocks = D // BLOCK
    tokens_here = inputs.shape[0]
    grad_scale = 1.0 / math.sqrt(tokens_here * lax.axis_size("dp"))
    gate_live, gate_feat, gate_row = decode(gate_list[0], hidden_rows)
    up_live, up_feat, up_row = decode(up_list[0], hidden_rows)
    down_live, down_feat, down_row = decode(down_list[0], hidden_rows)
    whole_in, whole_cot = (
        lax.all_gather(inputs, "tensor", axis=1, tiled=True),
        lax.all_gather(cotangent, "tensor", axis=1, tiled=True),
    )
    input_blocks = whole_in.reshape(tokens_here, feat_blocks, BLOCK)
    gate_in = jnp.take(input_blocks, gate_feat, axis=1)
    up_in = jnp.take(input_blocks, up_feat, axis=1)
    gate_val = project_rows(gate_in, gate_w[0], one_hot(gate_row, hidden_rows, gate_live))
    up_val = project_rows(up_in, up_w[0], one_hot(up_row, hidden_rows, up_live))
    sigmoid_gate = jax.nn.sigmoid(gate_val)
    active = gate_val * sigmoid_gate
    hidden = (active * up_val).astype(jnp.bfloat16)
    cot_blocks = whole_cot.reshape(tokens_here, feat_blocks, BLOCK)
    down_cot = jnp.take(cot_blocks, down_feat, axis=1)
    hidden_down = jnp.take(hidden, down_row, axis=1)
    down_part = jnp.einsum("tkc,khc->tkh", down_cot, down_w[0], preferred_element_type=jnp.float32)
    grad_hidden = select_sum(down_part, one_hot(down_row, hidden_rows, down_live))
    down_term = weight_term(
        jnp.einsum("tkh,tkc->khc", hidden_down, down_cot, preferred_element_type=jnp.float32),
        grad_scale,
        down_live,
    )
    grad_gate = (
        grad_hidden * up_val * sigmoid_gate * (1.0 + gate_val * (1.0 - sigmoid_gate))
    ).astype(jnp.bfloat16)
    grad_up = (grad_hidden * active).astype(jnp.bfloat16)
    gate_back = jnp.take(grad_gate, gate_row, axis=1)
    up_back = jnp.take(grad_up, up_row, axis=1)
    gate_term = weight_term(
        jnp.einsum("tkc,tkh->kch", gate_in, gate_back, preferred_element_type=jnp.float32),
        grad_scale,
        gate_live,
    )
    up_term = weight_term(
        jnp.einsum("tkc,tkh->kch", up_in, up_back, preferred_element_type=jnp.float32),
        grad_scale,
        up_live,
    )
    back_gate = jnp.einsum("tkh,kch->tkc", gate_back, gate_w[0], preferred_element_type=jnp.float32)
    back_up = jnp.einsum("tkh,kch->tkc", up_back, up_w[0], preferred_element_type=jnp.float32)
    partial_sum = select_sum(back_gate, one_hot(gate_feat, feat_blocks, gate_live))
    partial_sum = partial_sum + select_sum(back_up, one_hot(up_feat, feat_blocks, up_live))
    pieces = partial_sum.astype(jnp.bfloat16).reshape(tokens_here, tensor_size, D // tensor_size)
    summed = add_sources(lax.all_to_all(pieces, "tensor", split_axis=1, concat_axis=1, tiled=True))
    grad_x = summed.astype(jnp.bfloat16)
    gate_sum, up_sum, down_sum = (
        lax.psum_scatter(
            gate_term.astype(jnp.bfloat16), "dp", scatter_dimension=2, tiled=True
        ).astype(jnp.float32),
        lax.psum_scatter(
            up_term.astype(jnp.bfloat16), "dp", scatter_dimension=2, tiled=True
        ).astype(jnp.float32),
        lax.psum_scatter(
            down_term.astype(jnp.bfloat16), "dp", scatter_dimension=2, tiled=True
        ).astype(jnp.float32),
    )
    return (
        grad_x,
        gate_sum.astype(jnp.bfloat16),
        up_sum.astype(jnp.bfloat16),
        down_sum.astype(jnp.bfloat16),
    )


def pair_tables(lists, hidden_rows, length):
    slots = lists.shape[1]
    live = lists >= 0
    clamped = jnp.maximum(lists, 0)
    feat, row = clamped // hidden_rows, clamped % hidden_rows
    hot = (row[:, :, None] == jnp.arange(hidden_rows)) & live[:, :, None]
    counts = jnp.sum(hot.astype(jnp.int32), axis=1)
    padded = (counts + 1) // 2 * 2
    order = jnp.arange(slots)
    same = (row[:, :, None] == row[:, None, :]) & (order[None, :] < order[:, None])
    rank = jnp.sum(same.astype(jnp.int32), axis=2)
    before = jnp.arange(hidden_rows) < row[:, :, None]
    start = jnp.sum(jnp.where(before, padded[:, None, :], 0), axis=2)
    place = jnp.where(live, start + rank, -1)
    here = place[:, :, None] == jnp.arange(length)
    slot = jnp.sum(jnp.where(here, (order - slots)[None, :, None], 0), axis=1) + slots
    feat_at = jnp.sum(jnp.where(here, feat[:, :, None], 0), axis=1)
    row_at = jnp.sum(jnp.where(here, row[:, :, None], 0), axis=1)
    pairs = jnp.sum(padded, axis=1) // 2
    living = jnp.sum(live.astype(jnp.int32), axis=1)
    return jnp.concatenate([slot, feat_at, row_at], axis=0), jnp.concatenate([pairs, living])


def nt_dot(a, b):
    return lax.dot_general(a, b, (((1,), (1,)), ((), ())), preferred_element_type=F32)


def layer_kernel(
    hidden_rows, feat_blocks, groups, tok, grad_scale,
    counts, tables, lists, in_hbm, cot_hbm, gate_hbm, up_hbm, down_hbm,
    part_ref, ggw_ref, guw_ref, gdw_ref,
    xin, cot, gw, uw, dw, gate, up, gh, gg, gu, hid, xt, ht, dense, back_g, back_u, sems,
):
    slots = lists.shape[1]
    tokens = groups * tok
    rows = BLOCK // groups
    pick = groups
    me = lax.axis_index("dp")
    copies = [
        pltpu.make_async_copy(src, dst, sems.at[i])
        for i, (src, dst) in enumerate((
            (in_hbm, xin),
            (gate_hbm.at[0], gw.at[pl.ds(0, slots)]),
            (up_hbm.at[0], uw.at[pl.ds(0, slots)]),
            (cot_hbm, cot),
            (down_hbm.at[0], dw.at[pl.ds(0, slots)]),
        ))
    ]
    for copy in copies:
        copy.start()
    blank = jnp.zeros((BLOCK, BLOCK), BF16)
    gw[slots] = blank
    uw[slots] = blank
    dw[slots] = blank

    @pl.loop(0, hidden_rows)
    def _(h):
        zero = jnp.zeros((tokens, BLOCK), F32)
        gate[h] = zero
        up[h] = zero
        gh[h] = zero

    @pl.loop(0, feat_blocks)
    def _(d):
        zero = jnp.zeros((tok, BLOCK), F32)
        back_g[d] = zero
        back_u[d] = zero

    for copy in copies:
        copy.wait()

    pairs = jnp.maximum(jnp.maximum(counts[0], counts[1]), counts[2])

    @pl.loop(0, (pairs + UNROLL - 1) // UNROLL)
    def _(t):
        for u in range(UNROLL):
            a = 2 * (t * UNROLL + u)
            b = a + 1
            for i, (acts, w, acc) in enumerate(((xin, gw, gate), (xin, uw, up), (cot, dw, gh))):
                left = jnp.concatenate([acts[tables[3 + i, a]], acts[tables[3 + i, b]]], axis=1)
                one, two = w[tables[i, a]], w[tables[i, b]]
                h = tables[6 + i, a]
                if i < 2:
                    got = jnp.dot(
                        left, jnp.concatenate([one, two], axis=0), preferred_element_type=F32
                    )
                else:
                    got = nt_dot(left, jnp.concatenate([one, two], axis=1))
                acc[h] += got

    @pl.loop(0, hidden_rows)
    def _(h):
        @pl.loop(0, tokens // 128)
        def _(r):
            at = pl.ds(pl.multiple_of(r * 128, 128), 128)
            g, u, y = gate[h, at], up[h, at], gh[h, at]
            sig = 1.0 / (1.0 + jnp.exp(-g))
            act = g * sig
            hid[h, at] = (act * u).astype(BF16)
            gg[h, at] = (y * u * sig * (1.0 + g * (1.0 - sig))).astype(BF16)
            gu[h, at] = (y * act).astype(BF16)

    own = pl.ds(pl.multiple_of(me * tok, tok), tok)
    living = jnp.maximum(counts[3], counts[4])

    @pl.loop(0, (living + BACK_UNROLL - 1) // BACK_UNROLL)
    def _(t):
        for u in range(BACK_UNROLL):
            k = t * BACK_UNROLL + u
            for i, (grad, w, acc) in enumerate(((gg, gw, back_g), (gu, uw, back_u))):
                e = lists[i, k]
                block = w[jnp.where(e >= 0, k, slots)]
                e = jnp.maximum(e, 0)
                acc[e // hidden_rows] += nt_dot(grad[e % hidden_rows, own], block)

    @pl.loop(0, feat_blocks)
    def _(d):
        part_ref[d] = (back_g[d] + back_u[d]).astype(BF16)

    line = lax.broadcasted_iota(jnp.int32, (pick * BLOCK, BLOCK), 0)
    lane = lax.broadcasted_iota(jnp.int32, (pick * BLOCK, BLOCK), 1)
    want = (lane // rows) * BLOCK + me * rows + lane % rows
    chooser = jnp.where(line == want, 1.0, 0.0).astype(BF16)

    def own_rows(src, dst, count):
        @pl.loop(0, count // pick)
        def _(g):
            wide = jnp.concatenate([src[g * pick + q] for q in range(pick)], axis=1)
            chosen = jnp.dot(wide, chooser, preferred_element_type=F32)
            at = pl.ds(pl.multiple_of(g * BLOCK, BLOCK), BLOCK)
            dst[at, :] = chosen.T.astype(BF16)

    own_rows(xin, xt, feat_blocks)
    own_rows(hid, ht, hidden_rows)

    def all_products(left, right, count):
        @pl.loop(0, count // 2)
        def _(n):
            two = jnp.concatenate([right[2 * n], right[2 * n + 1]], axis=1)
            got = jnp.dot(left[...], two, preferred_element_type=F32) * grad_scale
            got = got.astype(BF16)
            per = left.shape[0] // rows
            for s in range(2):
                dense[pl.ds((2 * n + s) * per, per)] = got[:, s * BLOCK:(s + 1) * BLOCK].reshape(
                    per, rows, BLOCK
                )

    def keep_live(i, out, by_feat):
        @pl.loop(0, slots // SLOT_UNROLL)
        def _(t):
            for u in range(SLOT_UNROLL):
                k = t * SLOT_UNROLL + u
                e = lists[i, k]
                c = jnp.maximum(e, 0)
                d, h = c // hidden_rows, c % hidden_rows
                at = d * hidden_rows + h if by_feat else h * feat_blocks + d
                block = dense[at]
                out[0, k] = jnp.where(e >= 0, block, jnp.zeros_like(block))

    all_products(xt, gg, hidden_rows)
    keep_live(0, ggw_ref, False)
    all_products(xt, gu, hidden_rows)
    keep_live(1, guw_ref, False)
    all_products(ht, cot, feat_blocks)
    keep_live(2, gdw_ref, True)


def layer(whole_in, whole_cot, gate_w, up_w, down_w, lists, tables, counts, hidden_rows, groups):
    feat_blocks, tokens, _ = whole_in.shape
    slots = lists.shape[1]
    tok = tokens // groups
    rows = BLOCK // groups
    grad_scale = 1.0 / math.sqrt(tokens)
    smem = pl.BlockSpec(memory_space=pltpu.SMEM)
    vmem = pl.BlockSpec(memory_space=pltpu.VMEM)
    hbm = pl.BlockSpec(memory_space=pl.ANY)
    weights = pltpu.VMEM((slots + 1, BLOCK, BLOCK), BF16)
    acts = pltpu.VMEM((feat_blocks, tokens, BLOCK), BF16)
    wide = pltpu.VMEM((hidden_rows, tokens, BLOCK), F32)
    narrow = pltpu.VMEM((hidden_rows, tokens, BLOCK), BF16)
    grad = jax.ShapeDtypeStruct((1, slots, rows, BLOCK), BF16)
    back = pltpu.VMEM((feat_blocks, tok, BLOCK), F32)
    return pl.pallas_call(
        functools.partial(layer_kernel, hidden_rows, feat_blocks, groups, tok, grad_scale),
        out_shape=(jax.ShapeDtypeStruct((feat_blocks, tok, BLOCK), BF16), grad, grad, grad),
        in_specs=[smem, smem, smem, hbm, hbm, hbm, hbm, hbm],
        out_specs=[vmem] * 4,
        scratch_shapes=[
            acts, acts, weights, weights, weights, wide, wide, wide, narrow, narrow, narrow,
            pltpu.VMEM((feat_blocks * rows, tokens), BF16),
            pltpu.VMEM((hidden_rows * rows, tokens), BF16),
            pltpu.VMEM((feat_blocks * hidden_rows, rows, BLOCK), BF16),
            back, back,
            pltpu.SemaphoreType.DMA((5,)),
        ],
        compiler_params=pltpu.CompilerParams(vmem_limit_bytes=60 * 1024 * 1024),
        name="layer",
    )(counts, tables, lists, whole_in, whole_cot, gate_w, up_w, down_w)


def on_device(inputs, cotangent, gate_w, up_w, down_w, gate_list, up_list, down_list):
    tensor_size, groups = lax.axis_size("tensor"), lax.axis_size("dp")
    hidden_rows = FF // (BLOCK * tensor_size)
    tok, width = inputs.shape
    mine = width // BLOCK
    slots = gate_list.shape[1]
    lists = jnp.concatenate([gate_list, up_list, down_list], axis=0)
    step = 2 * UNROLL
    length = (slots + hidden_rows + step - 1) // step * step
    tables, counts = pair_tables(lists, hidden_rows, length)

    def whole(x):
        x = x.reshape(tok, mine, BLOCK).transpose(1, 0, 2)
        x = lax.all_gather(x, "tensor", axis=0, tiled=True)
        return lax.all_gather(x, "dp", axis=1, tiled=True)

    part, ggw, guw, gdw = layer(
        whole(inputs), whole(cotangent), gate_w, up_w, down_w, lists, tables, counts,
        hidden_rows, groups,
    )
    pieces = part.reshape(tensor_size, mine, tok, BLOCK)
    got = lax.all_to_all(pieces, "tensor", split_axis=0, concat_axis=0, tiled=True)
    summed = jnp.sum(got.astype(F32), axis=0).astype(BF16)
    grad_x = summed.transpose(1, 0, 2).reshape(tok, width)
    return grad_x, ggw, guw, gdw


def fits(mesh):
    return BLOCK // mesh.shape["dp"] >= 16


def solution(mesh):
    return jax.shard_map(
        on_device if fits(mesh) else plain_on_device,
        mesh=mesh,
        in_specs=(
            P("dp", "tensor"),
            P("dp", "tensor"),
            P("tensor", None, None, None),
            P("tensor", None, None, None),
            P("tensor", None, None, None),
            P("tensor", None),
            P("tensor", None),
            P("tensor", None),
        ),
        out_specs=(
            P("dp", "tensor"),
            P("tensor", None, "dp", None),
            P("tensor", None, "dp", None),
            P("tensor", None, "dp", None),
        ),
        check_vma=False,
    )
```

profile of v0, /device:TPU:0, one launch (start us, length us, event | category | flops | bytes accessed | tf_op | source)
XLA Modules:
  0.0 259.0 jit_solution(3597877379397633492)
XLA Ops:
  7.2 0.0 copy-start
  7.2 0.0 copy-start.1
  7.2 0.0 copy-start.2
  7.2 0.0 all-gather.5.cloned.1.call-start
  7.2 1.0 copy.26
  8.3 0.8 copy.27
  9.0 0.0 all-gather.5.cloned.1.call-update
  9.1 0.0 all-gather.9.cloned.1.call-start
  9.1 1.0 copy.28
  10.1 0.8 copy.29
  10.9 0.0 all-gather.9.cloned.1.call-update
  10.9 0.0 all-gather.7.cloned.1.call-start
  11.0 24.0 %all-gather.5.cloned.1.call-done = bf16[32,128,128]{2,1,0:T(8,128)(2,1)} async-done(((bf16[4,128,128]{2,1,0:T(8,128)(2,1)}), bf16[32,128,128]{2,1,0:T(8,128)(2,1)}) %all-gather.5.cloned.1.call-update) | async-done | bytes 1048592 | tf_op jit(solution)/shard_map/all_gather | solution.py:338
  35.0 0.0 all-gather.7.cloned.1.call-update
  35.1 0.0 all-gather.11.cloned.1.call-start
  35.1 23.9 %all-gather.9.cloned.1.call-done = bf16[32,128,128]{2,1,0:T(8,128)(2,1)} async-done(((bf16[4,128,128]{2,1,0:T(8,128)(2,1)}), bf16[32,128,128]{2,1,0:T(8,128)(2,1)}) %all-gather.9.cloned.1.call-update) | async-done | bytes 1048592 | tf_op jit(solution)/shard_map/all_gather | solution.py:338
  59.0 0.0 all-gather.11.cloned.1.call-update
  59.0 0.0 copy-done
  59.0 0.0 copy-done.1
  59.0 0.0 copy-done.2
  59.0 0.7 pad_add_fusion.1
  59.7 0.1 convert_reduce_fusion.1
  59.9 0.1 fusion.5
  60.0 0.6 pad_add_fusion.2.counts
  60.6 0.1 select_reduce_fusion.3
  60.7 0.2 convert_reduce_fusion
  60.9 0.2 select_reduce_fusion.2
  61.1 0.6 pad_add_fusion.tables
  61.8 51.4 %all-gather.7.cloned.1.call-done.in_hbm = bf16[32,512,128]{2,1,0:T(8,128)(2,1)} async-done(((bf16[32,128,128]{2,1,0:T(8,128)(2,1)}), bf16[32,512,128]{2,1,0:T(8,128)(2,1)}) %all-gather.7.cloned.1.call-update) | async-done | bytes 4194320 | tf_op jit(solution)/shard_map/all_gather | solution.py:339
  113.2 54.4 %all-gather.11.cloned.1.call-done.cot_hbm = bf16[32,512,128]{2,1,0:T(8,128)(2,1)} async-done(((bf16[32,128,128]{2,1,0:T(8,128)(2,1)}), bf16[32,512,128]{2,1,0:T(8,128)(2,1)}) %all-gather.11.cloned.1.call-update) | async-done | bytes 4194320 | tf_op jit(solution)/shard_map/all_gather | solution.py:339
  167.6 52.5 %layer.1 = (bf16[32,128,128]{2,1,0:T(8,128)(2,1)}, bf16[1,96,32,128]{3,2,1,0:T(8,128)(2,1)}, bf16[1,96,32,128]{3,2,1,0:T(8,128)(2,1)}, bf16[1,96,32,128]{3,2,1,0:T(8,128)(2,1)}) custom-call(s32[6]{0:T(128)} %pad_add_fusion.2.counts, s32[9,112]{1,0:T(8,128)} %pad_add_fusion.tables, s32[3,96]{1,0:T(4,128)} %get-tuple-element.27.lists, ...), custom_call_target="tpu_custom_call" | custom-call | tf_op jit(solution)/shard_map/layer/pallas_call | solution.py:307
  220.2 31.2 %all_to_all.5 = bf16[8,4,128,128]{3,2,1,0:T(8,128)(2,1)S(1)} all-to-all(bf16[8,4,128,128]{3,2,1,0:T(8,128)(2,1)} %bitcast.9), channel_id=1, replica_groups=mesh['dp'=4,'tensor'=8] {'tensor'}, dimensions={0} | all-to-all | bytes 2097152 | tf_op jit(solution)/shard_map/all_to_all | solution.py:346
  251.4 0.1 reduce_sum.92
  251.5 0.1 copy.30
  251.7 0.8 copy.31
  (5 shorter events, 0.0 us)
Async XLA Ops:
  7.2 51.8 %copy-start = (s32[1,96]{1,0:T(1,128)S(1)}, s32[1,96]{1,0:T(1,128)}, u32[]{:S(2)}) copy-start(s32[1,96]{1,0:T(1,128)} %param.15) | copy-start | bytes 1156
  7.2 51.8 %copy-start.1 = (s32[1,96]{1,0:T(1,128)S(1)}, s32[1,96]{1,0:T(1,128)}, u32[]{:S(2)}) copy-start(s32[1,96]{1,0:T(1,128)} %param.14) | copy-start | bytes 1156
  7.2 51.8 %copy-start.2 = (s32[1,96]{1,0:T(1,128)S(1)}, s32[1,96]{1,0:T(1,128)}, u32[]{:S(2)}) copy-start(s32[1,96]{1,0:T(1,128)} %param.13) | copy-start | bytes 1156
  7.2 27.8 %all-gather.5.cloned.1.call-start = ((), (), s32[]{:S(2)}) async-start(), calls=%async_computation.1 | async-start | bytes 1179648 | tf_op jit(solution)/shard_map/all_gather | solution.py:338
  9.1 49.9 %all-gather.9.cloned.1.call-start = ((), (), s32[]{:S(2)}) async-start(), calls=%async_computation.3 | async-start | bytes 1179648 | tf_op jit(solution)/shard_map/all_gather | solution.py:338
  10.9 102.2 %all-gather.7.cloned.1.call-start = ((), (), s32[]{:S(2)}) async-start(), calls=%async_computation.2 | async-start | bytes 5242880 | tf_op jit(solution)/shard_map/all_gather | solution.py:339
  35.1 132.6 %all-gather.11.cloned.1.call-start = ((), (), s32[]{:S(2)}) async-start(), calls=%async_computation.4 | async-start | bytes 5242880 | tf_op jit(solution)/shard_map/all_gather | solution.py:339
Sparse Core Ops, SparseCore 0:
  10.2 24.7 all-gather.4
  37.2 21.7 all-gather.8
  60.8 52.3 all-gather.6
  114.9 52.6 all-gather.10
where the time goes:
time: 259 us
  waiting for transfers between devices  154 us (59%)
  Pallas kernels  52.5 us (20%)
  blocking collectives  31.2 us (12%)
  between operations  13.9 us (5%)
  local copies, waits for them, and re-layouts  4.51 us (2%)
  other arithmetic  2.86 us (1%)
    all_gather x2, waiting for transfers between devices, whole(): return lax.all_gather(x, 'dp', axis=1, tiled=True)  106 us
    pallas_call x1, Pallas kernels, layer(): pl.pallas_call(functools.partial(layer_kernel, hidden_rows, feat_blocks,...  52.5 us
    all_gather x2, waiting for transfers between devices, whole(): x = lax.all_gather(x, 'tensor', axis=0, tiled=True)  47.9 us
    all_to_all x1, blocking collectives, on_device(): lax.all_to_all(pieces, 'tensor', split_axis=0, concat_axis=0, tiled=True)  31.2 us
  transfers between devices with their start and end apart: 4, of which 4 were waited for; matrix products, arithmetic and copies ran while one was open for 2% of the time, Pallas kernels for 0%

commit v1 on v0

--- a/solution.py
+++ b/solution.py
@@ -151,7 +151,7 @@
 
 def layer_kernel(
     hidden_rows, feat_blocks, groups, tok, grad_scale,
-    counts, tables, lists, in_hbm, cot_hbm, gate_hbm, up_hbm, down_hbm,
+    counts, tables, lists, both_hbm, gate_hbm, up_hbm, down_hbm,
     part_ref, ggw_ref, guw_ref, gdw_ref,
     xin, cot, gw, uw, dw, gate, up, gh, gg, gu, hid, xt, ht, dense, back_g, back_u, sems,
 ):
@@ -163,10 +163,10 @@
     copies = [
         pltpu.make_async_copy(src, dst, sems.at[i])
         for i, (src, dst) in enumerate((
-            (in_hbm, xin),
+            (both_hbm.at[0], xin),
             (gate_hbm.at[0], gw.at[pl.ds(0, slots)]),
             (up_hbm.at[0], uw.at[pl.ds(0, slots)]),
-            (cot_hbm, cot),
+            (both_hbm.at[1], cot),
             (down_hbm.at[0], dw.at[pl.ds(0, slots)]),
         ))
     ]
@@ -289,8 +289,8 @@
     keep_live(2, gdw_ref, True)
 
 
-def layer(whole_in, whole_cot, gate_w, up_w, down_w, lists, tables, counts, hidden_rows, groups):
-    feat_blocks, tokens, _ = whole_in.shape
+def layer(both, gate_w, up_w, down_w, lists, tables, counts, hidden_rows, groups):
+    _, feat_blocks, tokens, _ = both.shape
     slots = lists.shape[1]
     tok = tokens // groups
     rows = BLOCK // groups
@@ -307,7 +307,7 @@
     return pl.pallas_call(
         functools.partial(layer_kernel, hidden_rows, feat_blocks, groups, tok, grad_scale),
         out_shape=(jax.ShapeDtypeStruct((feat_blocks, tok, BLOCK), BF16), grad, grad, grad),
-        in_specs=[smem, smem, smem, hbm, hbm, hbm, hbm, hbm],
+        in_specs=[smem, smem, smem, hbm, hbm, hbm, hbm],
         out_specs=[vmem] * 4,
         scratch_shapes=[
             acts, acts, weights, weights, weights, wide, wide, wide, narrow, narrow, narrow,
@@ -319,7 +319,195 @@
         ],
         compiler_params=pltpu.CompilerParams(vmem_limit_bytes=60 * 1024 * 1024),
         name="layer",
-    )(counts, tables, lists, whole_in, whole_cot, gate_w, up_w, down_w)
+    )(counts, tables, lists, both, gate_w, up_w, down_w)
+
+
+def gather_kernel(
+    span, x_ref, cot_ref, out, own, local, col_sent, cross_sent, side_sent, col_got, cross_got, side_got
+):
+    tok = x_ref.shape[0]
+    mine = x_ref.shape[1] // BLOCK
+    p, t = lax.axis_index("dp"), lax.axis_index("tensor")
+    z, core = t // 2, t % 2
+    over_x, over_y, corner = p + 1 - 2 * (p % 2), (p + 2) % 4, 3 - p
+    other = t + 1 - 2 * core
+
+    barrier = pltpu.get_barrier_semaphore()
+
+    def greet(device):
+        pl.semaphore_signal(barrier, inc=1, device_id=device, device_id_type=pl.DeviceIdType.MESH)
+
+    greet((over_x, t))
+    greet((over_y, t))
+    greet((p, other))
+
+    @pl.when(z > 0)
+    def _():
+        greet((p, t - 2))
+
+    @pl.when(z < span - 1)
+    def _():
+        greet((p, t + 2))
+
+    for b in range(mine):
+        own[0, b] = x_ref[:, b * BLOCK:(b + 1) * BLOCK]
+        own[1, b] = cot_ref[:, b * BLOCK:(b + 1) * BLOCK]
+
+    inside = (z > 0) & (z < span - 1)
+
+    @pl.when(inside)
+    def _():
+        pl.semaphore_wait(barrier, 5)
+
+    @pl.when(jnp.logical_not(inside))
+    def _():
+        pl.semaphore_wait(barrier, 4)
+
+    def region(group, level, which, array=None):
+        blocks = pl.ds((level * 2 + which) * mine, mine)
+        rows = pl.ds(pl.multiple_of(group * tok, tok), tok)
+        if array is None:
+            return out.at[:, blocks, rows]
+        return out.at[array, blocks, rows]
+
+    def copy(src, dst, sent, got, device):
+        return pltpu.make_async_remote_copy(
+            src_ref=src, dst_ref=dst, send_sem=sent, recv_sem=got,
+            device_id=device, device_id_type=pl.DeviceIdType.MESH,
+        )
+
+    def along(level, way, src=None):
+        here = region(p, level, core)
+        return copy(
+            here if src is None else src, here, col_sent.at[way, level], col_got.at[level],
+            (p, t + 2 if way == 0 else t - 2),
+        )
+
+    def across(level, kind, src=None):
+        if kind < 2:
+            here = region(p, level, core)
+        elif kind == 2:
+            here = region(over_x, level, core, 0)
+        else:
+            here = region(over_y, level, core, 1)
+        to = over_x if kind in (0, 3) else over_y
+        return copy(
+            here if src is None else src, here, cross_sent.at[kind, level], cross_got.at[kind, level],
+            (to, t),
+        )
+
+    def aside(level, kind, src=None, which=core):
+        here = (
+            region(p, level, which), region(over_x, level, which), region(over_y, level, which),
+            region(corner, level, which, 0), region(corner, level, which, 1),
+        )[kind]
+        return copy(
+            here if src is None else src, here, side_sent.at[kind, level], side_got.at[kind, level],
+            (p, other),
+        )
+
+    def column(level, sign):
+        src = None
+        if sign == 0:
+            src = own
+        else:
+            along(level, 0).wait_recv()
+        if sign <= 0:
+            @pl.when(z < span - 1)
+            def _():
+                along(level, 0, src).start()
+        if sign >= 0:
+            @pl.when(z > 0)
+            def _():
+                along(level, 1, src).start()
+        across(level, 0, src).start()
+        across(level, 1, src).start()
+        aside(level, 0, src).start()
+
+    def cross(level, sign):
+        copy(
+            region(over_x, level, core), region(over_x, level, core), cross_sent.at[0, level],
+            cross_got.at[0, level], (over_x, t),
+        ).wait_recv()
+        across(level, 2).start()
+        aside(level, 1).start()
+        copy(
+            region(over_y, level, core), region(over_y, level, core), cross_sent.at[1, level],
+            cross_got.at[1, level], (over_y, t),
+        ).wait_recv()
+        across(level, 3).start()
+        aside(level, 2).start()
+
+    def diagonal(level, sign):
+        for kind in (2, 3):
+            here = region(corner, level, core, kind - 2)
+            copy(
+                here, here, cross_sent.at[kind, level], cross_got.at[kind, level],
+                (over_y if kind == 2 else over_x, t),
+            ).wait_recv()
+            aside(level, kind + 1).start()
+
+    keep = pltpu.make_async_copy(own, region(p, z, core), local)
+    keep.start()
+
+    def at_distance(step, action):
+        if step < 0 or step >= span:
+            return
+        if step == 0:
+            action(z, 0)
+            return
+
+        @pl.when(z >= step)
+        def _():
+            action(z - step, -1)
+
+        @pl.when(z + step < span)
+        def _():
+            action(z + step, 1)
+
+    for step in range(span + 2):
+        at_distance(step, column)
+        at_distance(step - 1, cross)
+        at_distance(step - 2, diagonal)
+
+    keep.wait()
+    for level in range(span):
+        for kind in range(4):
+            across(level, kind).wait_send()
+        for kind in range(5):
+            aside(level, kind).wait_send()
+            aside(level, kind, which=1 - core).wait_recv()
+
+        @pl.when((z >= level) & (z < span - 1))
+        def _():
+            along(level, 0).wait_send()
+
+        @pl.when((z <= level) & (z > 0))
+        def _():
+            along(level, 1).wait_send()
+
+
+def gather(inputs, cotangent, tensor_size, groups):
+    tok, width = inputs.shape
+    mine, span = width // BLOCK, tensor_size // 2
+    vmem = pl.BlockSpec(memory_space=pltpu.VMEM)
+    dma = pltpu.SemaphoreType.DMA
+    return pl.pallas_call(
+        functools.partial(gather_kernel, span),
+        out_shape=jax.ShapeDtypeStruct((2, mine * tensor_size, tok * groups, BLOCK), BF16),
+        in_specs=[vmem, vmem],
+        out_specs=pl.BlockSpec(memory_space=pl.ANY),
+        scratch_shapes=[
+            pltpu.VMEM((2, mine, tok, BLOCK), BF16),
+            dma(()),
+            dma((2, span)), dma((4, span)), dma((5, span)),
+            dma((span,)), dma((4, span)), dma((5, span)),
+        ],
+        compiler_params=pltpu.CompilerParams(
+            collective_id=0, has_side_effects=True, vmem_limit_bytes=32 * 1024 * 1024
+        ),
+        name="gather",
+    )(inputs, cotangent)
 
 
 def on_device(inputs, cotangent, gate_w, up_w, down_w, gate_list, up_list, down_list):
@@ -333,14 +521,9 @@
     length = (slots + hidden_rows + step - 1) // step * step
     tables, counts = pair_tables(lists, hidden_rows, length)
 
-    def whole(x):
-        x = x.reshape(tok, mine, BLOCK).transpose(1, 0, 2)
-        x = lax.all_gather(x, "tensor", axis=0, tiled=True)
-        return lax.all_gather(x, "dp", axis=1, tiled=True)
-
+    both = gather(inputs, cotangent, tensor_size, groups)
     part, ggw, guw, gdw = layer(
-        whole(inputs), whole(cotangent), gate_w, up_w, down_w, lists, tables, counts,
-        hidden_rows, groups,
+        both, gate_w, up_w, down_w, lists, tables, counts, hidden_rows, groups
     )
     pieces = part.reshape(tensor_size, mine, tok, BLOCK)
     got = lax.all_to_all(pieces, "tensor", split_axis=0, concat_axis=0, tiled=True)
@@ -350,7 +533,7 @@
 
 
 def fits(mesh):
-    return BLOCK // mesh.shape["dp"] >= 16
+    return mesh.shape["dp"] == 4 and mesh.shape["tensor"] >= 4
 
 
 def solution(mesh):

time: 259 us -> 137 us (0.53)
  waiting for transfers between devices: 154 us -> 0 us
  Pallas kernels: 52.5 us -> 84 us
  between operations: 13.9 us -> 0.69 us
  blocking collectives: 31.2 us -> 42.1 us
    all_gather x4 -> x0, waiting for transfers between devices: 154 us -> none  [the longest x2 106 us: whole(): return lax.all_gather(x, 'dp', axis=1, tiled=True)]
    pallas_call x0 -> x1, Pallas kernels: none -> 42.6 us  [gather(): pl.pallas_call(functools.partial(gather_kernel, span), out_shape=jax.Shap...]
    pallas_call x1, Pallas kernels: 52.5 us -> 41.4 us  [layer(): pl.pallas_call(functools.partial(layer_kernel, hidden_rows, feat_blocks,...]
    all_to_all x1, blocking collectives: 31.2 us -> 42.1 us  [on_device(): lax.all_to_all(pieces, 'tensor', split_axis=0, concat_axis=0, tiled=True)]
    unnamed x9 -> x7, local copies, waits for them, and re-layouts: 2.83 us -> 5.8 us
  transfers between devices with their start and end apart: 4 -> 0, of which waited for: 4 -> 0; matrix products, arithmetic and copies ran while one was open for 2% -> 0% of each run, Pallas kernels for 0% -> 0%
where the time goes in v1:
time: 137 us; the launch traced here: 136 us
  Pallas kernels  84 us (61%)
  blocking collectives  42.1 us (31%)
  local copies, waits for them, and re-layouts  5.93 us (4%)
  other arithmetic  3.66 us (3%)
    pallas_call x1, Pallas kernels, gather(): pl.pallas_call(functools.partial(gather_kernel, span), out_shape=jax.Shap...  42.6 us
    all_to_all x1, blocking collectives, on_device(): lax.all_to_all(pieces, 'tensor', split_axis=0, concat_axis=0, tiled=True)  42.1 us
    pallas_call x1, Pallas kernels, layer(): pl.pallas_call(functools.partial(layer_kernel, hidden_rows, feat_blocks,...  41.4 us
    unnamed x7, local copies, waits for them, and re-layouts  5.8 us

profile of v1, /device:TPU:0, one launch (start us, length us, event | category | flops | bytes accessed | tf_op | source)
XLA Modules:
  0.0 136.4 jit_solution(7178800695161457760)
XLA Ops:
  0.7 1.4 %pad_add_fusion.1 = (s32[3,96]{1,0:T(4,128)}, s32[3,96]{1,0:T(4,128)S(1)}, s32[3]{0:T(128)S(1)}, pred[3,96]{1,0:T(4,128)(4,1)S(1)}, s32[3,96]{1,0:T(4,128)S(1)}) fusion(s32[1,96]{1,0:T(1,128)} %param.15, s32[1,96]{1,0:T(1,128)} %param.14, s32[1,96]{1,0:T(1,128)} %param.13), kind=kLoop, calls=%fused_computation.20 | loop fusion | flops 5181 | bytes 4908 | tf_op jit(solution)/shard_map/concatenate | solution.py:519
  2.1 0.1 convert_reduce_fusion.1
  2.2 0.1 fusion.5
  2.4 0.1 select_reduce_fusion.3
  2.4 0.2 convert_reduce_fusion
  2.7 0.2 select_reduce_fusion.2
  2.9 0.7 pad_add_fusion.2.counts
  3.6 0.0 copy-start.1
  3.6 0.9 copy-done.1
  4.5 0.0 copy-start.2
  4.5 0.9 copy-done.2
  5.4 42.6 %gather.1.both_hbm = bf16[2,32,512,128]{3,2,1,0:T(8,128)(2,1)S(1)} custom-call(bf16[128,512]{1,0:T(8,128)(2,1)S(1)} %copy-done.1, bf16[128,512]{1,0:T(8,128)(2,1)S(1)} %copy-done.2), custom_call_target="tpu_custom_call" | custom-call | tf_op jit(solution)/shard_map/gather/pallas_call | solution.py:495
  48.0 0.0 copy-start
  48.0 3.2 %copy-done = bf16[2,32,512,128]{3,2,1,0:T(8,128)(2,1)} copy-done((bf16[2,32,512,128]{3,2,1,0:T(8,128)(2,1)}, bf16[2,32,512,128]{3,2,1,0:T(8,128)(2,1)S(1)}, u32[]{:S(2)}) %copy-start) | copy-done | bytes 8388632
  51.2 0.6 pad_add_fusion.tables
  51.8 41.4 %layer.1 = (bf16[32,128,128]{2,1,0:T(8,128)(2,1)}, bf16[1,96,32,128]{3,2,1,0:T(8,128)(2,1)}, bf16[1,96,32,128]{3,2,1,0:T(8,128)(2,1)}, bf16[1,96,32,128]{3,2,1,0:T(8,128)(2,1)}) custom-call(s32[6]{0:T(128)} %pad_add_fusion.2.counts, s32[9,112]{1,0:T(8,128)} %pad_add_fusion.tables, s32[3,96]{1,0:T(4,128)} %get-tuple-element.27.lists, ...), custom_call_target="tpu_custom_call" | custom-call | tf_op jit(solution)/shard_map/layer/pallas_call | solution.py:307
  93.2 42.1 %all_to_all.5 = bf16[8,4,128,128]{3,2,1,0:T(8,128)(2,1)S(1)} all-to-all(bf16[8,4,128,128]{3,2,1,0:T(8,128)(2,1)} %bitcast.3), channel_id=1, replica_groups=mesh['dp'=4,'tensor'=8] {'tensor'}, dimensions={0} | all-to-all | bytes 2097152 | tf_op jit(solution)/shard_map/all_to_all | solution.py:529
  135.4 0.1 reduce_sum.92
  135.5 0.1 copy.14
  135.6 0.8 copy.15
  (5 shorter events, 0.0 us)
Async XLA Ops:
  3.6 0.9 copy-start.1
  4.5 0.9 copy-start.2
  48.0 3.2 %copy-start = (bf16[2,32,512,128]{3,2,1,0:T(8,128)(2,1)}, bf16[2,32,512,128]{3,2,1,0:T(8,128)(2,1)S(1)}, u32[]{:S(2)}) copy-start(bf16[2,32,512,128]{3,2,1,0:T(8,128)(2,1)S(1)} %gather.1.both_hbm) | copy-start | bytes 25165828

commit v2 on v1

--- a/solution.py
+++ b/solution.py
@@ -11,7 +11,7 @@
 D = 4096
 FF = 16384
 BLOCK = 128
-UNROLL = 2
+UNROLL = 4
 BACK_UNROLL = 4
 SLOT_UNROLL = 8
 F32 = jnp.float32
@@ -150,15 +150,16 @@
 
 
 def layer_kernel(
-    hidden_rows, feat_blocks, groups, tok, grad_scale,
+    hidden_rows, feat_blocks, groups, tok, span,
     counts, tables, lists, both_hbm, gate_hbm, up_hbm, down_hbm,
-    part_ref, ggw_ref, guw_ref, gdw_ref,
-    xin, cot, gw, uw, dw, gate, up, gh, gg, gu, hid, xt, ht, dense, back_g, back_u, sems,
+    part_ref, gg_hbm, gu_hbm, xt_hbm, ht_hbm,
+    xin, cot, gw, uw, dw, gate, up, gh, gg, gu, hid, xt, ht, back_g, back_u, sems, out_sems,
 ):
     slots = lists.shape[1]
     tokens = groups * tok
     rows = BLOCK // groups
     pick = groups
+    mine = feat_blocks // (2 * span)
     me = lax.axis_index("dp")
     copies = [
         pltpu.make_async_copy(src, dst, sems.at[i])
@@ -190,27 +191,29 @@
         back_g[d] = zero
         back_u[d] = zero
 
-    for copy in copies:
+    def products(pairs, which):
+        @pl.loop(0, (pairs + UNROLL - 1) // UNROLL)
+        def _(t):
+            for u in range(UNROLL):
+                a = 2 * (t * UNROLL + u)
+                b = a + 1
+                for i, acts, w, acc in which:
+                    left = jnp.concatenate([acts[tables[3 + i, a]], acts[tables[3 + i, b]]], axis=1)
+                    one, two = w[tables[i, a]], w[tables[i, b]]
+                    if i < 2:
+                        found = jnp.dot(
+                            left, jnp.concatenate([one, two], axis=0), preferred_element_type=F32
+                        )
+                    else:
+                        found = nt_dot(left, jnp.concatenate([one, two], axis=1))
+                    acc[tables[6 + i, a]] += found
+
+    for copy in copies[:3]:
         copy.wait()
-
-    pairs = jnp.maximum(jnp.maximum(counts[0], counts[1]), counts[2])
-
-    @pl.loop(0, (pairs + UNROLL - 1) // UNROLL)
-    def _(t):
-        for u in range(UNROLL):
-            a = 2 * (t * UNROLL + u)
-            b = a + 1
-            for i, (acts, w, acc) in enumerate(((xin, gw, gate), (xin, uw, up), (cot, dw, gh))):
-                left = jnp.concatenate([acts[tables[3 + i, a]], acts[tables[3 + i, b]]], axis=1)
-                one, two = w[tables[i, a]], w[tables[i, b]]
-                h = tables[6 + i, a]
-                if i < 2:
-                    got = jnp.dot(
-                        left, jnp.concatenate([one, two], axis=0), preferred_element_type=F32
-                    )
-                else:
-                    got = nt_dot(left, jnp.concatenate([one, two], axis=1))
-                acc[h] += got
+    products(jnp.maximum(counts[0], counts[1]), ((0, xin, gw, gate), (1, xin, uw, up)))
+    for copy in copies[3:]:
+        copy.wait()
+    products(counts[2], ((2, cot, dw, gh),))
 
     @pl.loop(0, hidden_rows)
     def _(h):
@@ -224,6 +227,31 @@
             gg[h, at] = (y * u * sig * (1.0 + g * (1.0 - sig))).astype(BF16)
             gu[h, at] = (y * act).astype(BF16)
 
+    leaving = [
+        pltpu.make_async_copy(src, dst, out_sems.at[i])
+        for i, (src, dst) in enumerate(((gg, gg_hbm), (gu, gu_hbm), (xt, xt_hbm), (ht, ht_hbm)))
+    ]
+    leaving[0].start()
+    leaving[1].start()
+
+    line = lax.broadcasted_iota(jnp.int32, (pick * BLOCK, BLOCK), 0)
+    lane = lax.broadcasted_iota(jnp.int32, (pick * BLOCK, BLOCK), 1)
+    want = (lane // rows) * BLOCK + me * rows + lane % rows
+    chooser = jnp.where(line == want, 1.0, 0.0).astype(BF16)
+
+    def own_rows(src, dst, count):
+        @pl.loop(0, count // pick)
+        def _(g):
+            wide = jnp.concatenate([src[g * pick + q] for q in range(pick)], axis=1)
+            chosen = jnp.dot(wide, chooser, preferred_element_type=F32)
+            at = pl.ds(pl.multiple_of(g * BLOCK, BLOCK), BLOCK)
+            dst[at, :] = chosen.T.astype(BF16)
+
+    own_rows(xin, xt, feat_blocks)
+    own_rows(hid, ht, hidden_rows)
+    leaving[2].start()
+    leaving[3].start()
+
     own = pl.ds(pl.multiple_of(me * tok, tok), tok)
     living = jnp.maximum(counts[3], counts[4])
 
@@ -239,62 +267,18 @@
 
     @pl.loop(0, feat_blocks)
     def _(d):
-        part_ref[d] = (back_g[d] + back_u[d]).astype(BF16)
-
-    line = lax.broadcasted_iota(jnp.int32, (pick * BLOCK, BLOCK), 0)
-    lane = lax.broadcasted_iota(jnp.int32, (pick * BLOCK, BLOCK), 1)
-    want = (lane // rows) * BLOCK + me * rows + lane % rows
-    chooser = jnp.where(line == want, 1.0, 0.0).astype(BF16)
-
-    def own_rows(src, dst, count):
-        @pl.loop(0, count // pick)
-        def _(g):
-            wide = jnp.concatenate([src[g * pick + q] for q in range(pick)], axis=1)
-            chosen = jnp.dot(wide, chooser, preferred_element_type=F32)
-            at = pl.ds(pl.multiple_of(g * BLOCK, BLOCK), BLOCK)
-            dst[at, :] = chosen.T.astype(BF16)
-
-    own_rows(xin, xt, feat_blocks)
-    own_rows(hid, ht, hidden_rows)
-
-    def all_products(left, right, count):
-        @pl.loop(0, count // 2)
-        def _(n):
-            two = jnp.concatenate([right[2 * n], right[2 * n + 1]], axis=1)
-            got = jnp.dot(left[...], two, preferred_element_type=F32) * grad_scale
-            got = got.astype(BF16)
-            per = left.shape[0] // rows
-            for s in range(2):
-                dense[pl.ds((2 * n + s) * per, per)] = got[:, s * BLOCK:(s + 1) * BLOCK].reshape(
-                    per, rows, BLOCK
-                )
-
-    def keep_live(i, out, by_feat):
-        @pl.loop(0, slots // SLOT_UNROLL)
-        def _(t):
-            for u in range(SLOT_UNROLL):
-                k = t * SLOT_UNROLL + u
-                e = lists[i, k]
-                c = jnp.maximum(e, 0)
-                d, h = c // hidden_rows, c % hidden_rows
-                at = d * hidden_rows + h if by_feat else h * feat_blocks + d
-                block = dense[at]
-                out[0, k] = jnp.where(e >= 0, block, jnp.zeros_like(block))
-
-    all_products(xt, gg, hidden_rows)
-    keep_live(0, ggw_ref, False)
-    all_products(xt, gu, hidden_rows)
-    keep_live(1, guw_ref, False)
-    all_products(ht, cot, feat_blocks)
-    keep_live(2, gdw_ref, True)
-
-
-def layer(both, gate_w, up_w, down_w, lists, tables, counts, hidden_rows, groups):
+        owner, b = d // mine, d % mine
+        part_ref[owner % 2, owner // 2, b] = (back_g[d] + back_u[d]).astype(BF16)
+
+    for copy in leaving:
+        copy.wait()
+
+
+def layer(both, gate_w, up_w, down_w, lists, tables, counts, hidden_rows, groups, span):
     _, feat_blocks, tokens, _ = both.shape
     slots = lists.shape[1]
     tok = tokens // groups
     rows = BLOCK // groups
-    grad_scale = 1.0 / math.sqrt(tokens)
     smem = pl.BlockSpec(memory_space=pltpu.SMEM)
     vmem = pl.BlockSpec(memory_space=pltpu.VMEM)
     hbm = pl.BlockSpec(memory_space=pl.ANY)
@@ -302,20 +286,27 @@
     acts = pltpu.VMEM((feat_blocks, tokens, BLOCK), BF16)
     wide = pltpu.VMEM((hidden_rows, tokens, BLOCK), F32)
     narrow = pltpu.VMEM((hidden_rows, tokens, BLOCK), BF16)
-    grad = jax.ShapeDtypeStruct((1, slots, rows, BLOCK), BF16)
+    mine = feat_blocks // (2 * span)
+
+    def leaves(*shape):
+        return jax.ShapeDtypeStruct(shape, BF16)
+
     back = pltpu.VMEM((feat_blocks, tok, BLOCK), F32)
     return pl.pallas_call(
-        functools.partial(layer_kernel, hidden_rows, feat_blocks, groups, tok, grad_scale),
-        out_shape=(jax.ShapeDtypeStruct((feat_blocks, tok, BLOCK), BF16), grad, grad, grad),
+        functools.partial(layer_kernel, hidden_rows, feat_blocks, groups, tok, span),
+        out_shape=(
+            leaves(2, span, mine, tok, BLOCK),
+            leaves(hidden_rows, tokens, BLOCK), leaves(hidden_rows, tokens, BLOCK),
+            leaves(feat_blocks * rows, tokens), leaves(hidden_rows * rows, tokens),
+        ),
         in_specs=[smem, smem, smem, hbm, hbm, hbm, hbm],
-        out_specs=[vmem] * 4,
+        out_specs=[vmem, hbm, hbm, hbm, hbm],
         scratch_shapes=[
             acts, acts, weights, weights, weights, wide, wide, wide, narrow, narrow, narrow,
             pltpu.VMEM((feat_blocks * rows, tokens), BF16),
             pltpu.VMEM((hidden_rows * rows, tokens), BF16),
-            pltpu.VMEM((feat_blocks * hidden_rows, rows, BLOCK), BF16),
             back, back,
-            pltpu.SemaphoreType.DMA((5,)),
+            pltpu.SemaphoreType.DMA((5,)), pltpu.SemaphoreType.DMA((4,)),
         ],
         compiler_params=pltpu.CompilerParams(vmem_limit_bytes=60 * 1024 * 1024),
         name="layer",
@@ -504,17 +495,156 @@
             dma((span,)), dma((4, span)), dma((5, span)),
         ],
         compiler_params=pltpu.CompilerParams(
-            collective_id=0, has_side_effects=True, vmem_limit_bytes=32 * 1024 * 1024
+            collective_id=0, has_side_effects=True, vmem_limit_bytes=60 * 1024 * 1024
         ),
         name="gather",
     )(inputs, cotangent)
 
 
+def finish_kernel(
+    hidden_rows, feat_blocks, groups, span, grad_scale,
+    lists, part, gg_hbm, gu_hbm, xt_hbm, ht_hbm, both_hbm,
+    gx_ref, ggw_ref, guw_ref, gdw_ref,
+    gg, gu, xt, ht, cot, dense, pair_in, pair_sum, peer_in, loads, pair_sems, sent, got,
+):
+    slots = lists.shape[1]
+    rows = BLOCK // groups
+    mine = feat_blocks // (2 * span)
+    p, t = lax.axis_index("dp"), lax.axis_index("tensor")
+    z, core = t // 2, t % 2
+    other = t + 1 - 2 * core
+    load_gg, load_xt, load_gu, load_ht, load_cot = [
+        pltpu.make_async_copy(src, dst, loads.at[i])
+        for i, (src, dst) in enumerate((
+            (gg_hbm, gg), (xt_hbm, xt), (gu_hbm, gu), (ht_hbm, ht), (both_hbm.at[1], cot),
+        ))
+    ]
+
+    barrier = pltpu.get_barrier_semaphore()
+
+    def greet(device):
+        pl.semaphore_signal(barrier, inc=1, device_id=device, device_id_type=pl.DeviceIdType.MESH)
+
+    greet((p, other))
+    for step in range(1, span):
+        greet((p, (t + 2 * step) % (2 * span)))
+    for load in (load_gg, load_xt, load_gu, load_ht, load_cot):
+        load.start()
+    pl.semaphore_wait(barrier, span)
+
+    pair = pltpu.make_async_remote_copy(
+        src_ref=part.at[1 - core], dst_ref=pair_in, send_sem=pair_sems.at[0], recv_sem=pair_sems.at[1],
+        device_id=(p, other), device_id_type=pl.DeviceIdType.MESH,
+    )
+    pair.start()
+    pair.wait_recv()
+
+    def to_peer(step):
+        to = (z + step) % span
+        return pltpu.make_async_remote_copy(
+            src_ref=pair_sum.at[to], dst_ref=peer_in.at[z], send_sem=sent.at[step],
+            recv_sem=got.at[z], device_id=(p, to * 2 + core), device_id_type=pl.DeviceIdType.MESH,
+        )
+
+    for step in [*range(1, span), 0]:
+        to = (z + step) % span
+
+        @pl.loop(0, mine)
+        def _(b):
+            pair_sum[to, b] = (part[core, to, b].astype(F32) + pair_in[to, b].astype(F32)).astype(BF16)
+
+        if step:
+            to_peer(step).start()
+
+    def all_products(left, right, count):
+        @pl.loop(0, count // 2)
+        def _(n):
+            two = jnp.concatenate([right[2 * n], right[2 * n + 1]], axis=1)
+            found = jnp.dot(left[...], two, preferred_element_type=F32) * grad_scale
+            found = found.astype(BF16)
+            per = left.shape[0] // rows
+            for s in range(2):
+                dense[pl.ds((2 * n + s) * per, per)] = found[:, s * BLOCK:(s + 1) * BLOCK].reshape(
+                    per, rows, BLOCK
+                )
+
+    def keep_live(i, out, by_feat):
+        @pl.loop(0, slots // SLOT_UNROLL)
+        def _(n):
+            for u in range(SLOT_UNROLL):
+                k = n * SLOT_UNROLL + u
+                e = lists[i, k]
+                c = jnp.maximum(e, 0)
+                d, h = c // hidden_rows, c % hidden_rows
+                at = d * hidden_rows + h if by_feat else h * feat_blocks + d
+                block = dense[at]
+                out[0, k] = jnp.where(e >= 0, block, jnp.zeros_like(block))
+
+    load_gg.wait()
+    load_xt.wait()
+    all_products(xt, gg, hidden_rows)
+    keep_live(0, ggw_ref, False)
+    load_gu.wait()
+    all_products(xt, gu, hidden_rows)
+    keep_live(1, guw_ref, False)
+    load_ht.wait()
+    load_cot.wait()
+    all_products(ht, cot, feat_blocks)
+    keep_live(2, gdw_ref, True)
+
+    for step in range(1, span):
+        at = (z + step) % span
+        pltpu.make_async_remote_copy(
+            src_ref=pair_sum.at[at], dst_ref=peer_in.at[at], send_sem=sent.at[step],
+            recv_sem=got.at[at], device_id=(p, at * 2 + core), device_id_type=pl.DeviceIdType.MESH,
+        ).wait_recv()
+    for b in range(mine):
+        total = pair_sum[z, b].astype(F32)
+        for step in range(1, span):
+            total = total + peer_in[(z + step) % span, b].astype(F32)
+        gx_ref[:, b * BLOCK:(b + 1) * BLOCK] = total.astype(BF16)
+    pair.wait_send()
+    for step in range(1, span):
+        to_peer(step).wait_send()
+
+
+def finish(part, gg, gu, xt, ht, both, lists, tensor_size, groups):
+    hidden_rows, tokens, _ = gg.shape
+    feat_blocks = both.shape[1]
+    slots = lists.shape[1]
+    tok, rows, span = tokens // groups, BLOCK // groups, tensor_size // 2
+    mine = feat_blocks // tensor_size
+    smem = pl.BlockSpec(memory_space=pltpu.SMEM)
+    vmem = pl.BlockSpec(memory_space=pltpu.VMEM)
+    hbm = pl.BlockSpec(memory_space=pl.ANY)
+    dma = pltpu.SemaphoreType.DMA
+    grad = jax.ShapeDtypeStruct((1, slots, rows, BLOCK), BF16)
+    bound = pltpu.VMEM((span, mine, tok, BLOCK), BF16)
+    return pl.pallas_call(
+        functools.partial(
+            finish_kernel, hidden_rows, feat_blocks, groups, span, 1.0 / math.sqrt(tokens)
+        ),
+        out_shape=(jax.ShapeDtypeStruct((tok, mine * BLOCK), BF16), grad, grad, grad),
+        in_specs=[smem, vmem, hbm, hbm, hbm, hbm, hbm],
+        out_specs=[vmem] * 4,
+        scratch_shapes=[
+            pltpu.VMEM(gg.shape, BF16), pltpu.VMEM(gu.shape, BF16),
+            pltpu.VMEM(xt.shape, BF16), pltpu.VMEM(ht.shape, BF16),
+            pltpu.VMEM((feat_blocks, tokens, BLOCK), BF16),
+            pltpu.VMEM((feat_blocks * hidden_rows, rows, BLOCK), BF16),
+            bound, bound, bound,
+            dma((5,)), dma((2,)), dma((span,)), dma((span,)),
+        ],
+        compiler_params=pltpu.CompilerParams(
+            collective_id=1, has_side_effects=True, vmem_limit_bytes=60 * 1024 * 1024
+        ),
+        name="finish",
+    )(lists, part, gg, gu, xt, ht, both)
+
+
 def on_device(inputs, cotangent, gate_w, up_w, down_w, gate_list, up_list, down_list):
     tensor_size, groups = lax.axis_size("tensor"), lax.axis_size("dp")
     hidden_rows = FF // (BLOCK * tensor_size)
-    tok, width = inputs.shape
-    mine = width // BLOCK
     slots = gate_list.shape[1]
     lists = jnp.concatenate([gate_list, up_list, down_list], axis=0)
     step = 2 * UNROLL
@@ -522,14 +652,10 @@
     tables, counts = pair_tables(lists, hidden_rows, length)
 
     both = gather(inputs, cotangent, tensor_size, groups)
-    part, ggw, guw, gdw = layer(
-        both, gate_w, up_w, down_w, lists, tables, counts, hidden_rows, groups
-    )
-    pieces = part.reshape(tensor_size, mine, tok, BLOCK)
-    got = lax.all_to_all(pieces, "tensor", split_axis=0, concat_axis=0, tiled=True)
-    summed = jnp.sum(got.astype(F32), axis=0).astype(BF16)
-    grad_x = summed.transpose(1, 0, 2).reshape(tok, width)
-    return grad_x, ggw, guw, gdw
+    part, gg, gu, xt, ht = layer(
+        both, gate_w, up_w, down_w, lists, tables, counts, hidden_rows, groups, tensor_size // 2
+    )
+    return finish(part, gg, gu, xt, ht, both, lists, tensor_size, groups)
 
 
 def fits(mesh):

time: 137 us -> 114 us (0.83)
  blocking collectives: 42.1 us -> 0 us
  Pallas kernels: 84 us -> 102 us
    all_to_all x1 -> x0, blocking collectives: 42.1 us -> none  [on_device(): lax.all_to_all(pieces, 'tensor', split_axis=0, concat_axis=0, tiled=True)]
    pallas_call x0 -> x1, Pallas kernels: none -> 31.1 us  [finish(): pl.pallas_call(functools.partial(finish_kernel, hidden_rows, feat_blocks,...]
    pallas_call x1, Pallas kernels: 41.4 us -> 26.7 us  [layer(): pl.pallas_call(functools.partial(layer_kernel, hidden_rows, feat_blocks,...]
    pallas_call x1, Pallas kernels: 42.6 us -> 44.5 us  [gather(): pl.pallas_call(functools.partial(gather_kernel, span), out_shape=jax.Shap...]
    concatenate x1 -> x0, other arithmetic: 1.4 us -> none  [on_device(): lists = jnp.concatenate([gate_list, up_list, down_list], axis=0)]
    select_n x0 -> x1, other arithmetic: none -> 1.39 us  [pair_tables(): feat, row = (clamped // hidden_rows, clamped % hidden_rows)]
    unnamed x7 -> x6, local copies, waits for them, and re-layouts: 5.8 us -> 6.65 us
where the time goes in v2:
time: 114 us; the launch traced here: 113 us
  Pallas kernels  102 us (89%)
  local copies, waits for them, and re-layouts  6.65 us (6%)
  other arithmetic  3.43 us (3%)
    pallas_call x1, Pallas kernels, gather(): pl.pallas_call(functools.partial(gather_kernel, span), out_shape=jax.Shap...  44.5 us
    pallas_call x1, Pallas kernels, finish(): pl.pallas_call(functools.partial(finish_kernel, hidden_rows, feat_blocks,...  31.1 us
    pallas_call x1, Pallas kernels, layer(): pl.pallas_call(functools.partial(layer_kernel, hidden_rows, feat_blocks,...  26.7 us
    unnamed x6, local copies, waits for them, and re-layouts  6.65 us

profile of v2, /device:TPU:0, one launch (start us, length us, event | category | flops | bytes accessed | tf_op | source)
XLA Modules:
  0.0 113.1 jit_solution(6137432362601685540)
XLA Ops:
  0.6 1.4 %add_select_fusion = (s32[3,96]{1,0:T(4,128)S(1)}, s32[3,96]{1,0:T(4,128)S(1)}, s32[3]{0:T(128)S(1)}, pred[3,96]{1,0:T(4,128)(4,1)S(1)}, s32[3,96]{1,0:T(4,128)}) fusion(s32[1,96]{1,0:T(1,128)} %param.15, s32[1,96]{1,0:T(1,128)} %param.14, s32[1,96]{1,0:T(1,128)} %param.13), kind=kLoop, calls=%fused_computation.12 | loop fusion | flops 5181 | bytes 4908 | tf_op jit(solution)/shard_map/jit(floor_divide)/jit(_where)/select_n | solution.py:129
  2.0 0.1 convert_reduce_fusion.1
  2.2 0.1 fusion.5
  2.3 0.6 pad_add_fusion.2.counts
  2.9 0.1 select_reduce_fusion.3
  3.0 0.2 convert_reduce_fusion
  3.3 0.2 select_reduce_fusion.2
  3.5 0.6 pad_add_fusion.tables
  4.1 44.5 %gather.1.both_hbm = bf16[2,32,512,128]{3,2,1,0:T(8,128)(2,1)} custom-call(bf16[128,512]{1,0:T(8,128)(2,1)} %x_ref.1, bf16[128,512]{1,0:T(8,128)(2,1)} %cot_ref.1), custom_call_target="tpu_custom_call" | custom-call | tf_op jit(solution)/shard_map/gather/pallas_call | solution.py:486
  48.6 26.7 %layer.1 = (bf16[2,4,4,128,128]{4,3,2,1,0:T(8,128)(2,1)}, bf16[16,512,128]{2,1,0:T(8,128)(2,1)}, bf16[16,512,128]{2,1,0:T(8,128)(2,1)}, bf16[1024,512]{1,0:T(8,128)(2,1)}, bf16[512,512]{1,0:T(8,128)(2,1)}) custom-call(s32[6]{0:T(128)} %pad_add_fusion.2.counts, s32[9,112]{1,0:T(8,128)} %pad_add_fusion.tables, s32[3,96]{1,0:T(4,128)} %get-tuple-element.25.lists, ...), custom_call_target="tpu_custom_call" | custom-call | tf_op jit(solution)/shard_map/layer/pallas_call | solution.py:295
  75.3 31.1 %finish.1 = (bf16[128,512]{1,0:T(8,128)(2,1)}, bf16[1,96,32,128]{3,2,1,0:T(8,128)(2,1)}, bf16[1,96,32,128]{3,2,1,0:T(8,128)(2,1)}, bf16[1,96,32,128]{3,2,1,0:T(8,128)(2,1)}) custom-call(s32[3,96]{1,0:T(4,128)} %get-tuple-element.25.lists, bf16[2,4,4,128,128]{4,3,2,1,0:T(8,128)(2,1)} %get-tuple-element.9.part, ...), custom_call_target="tpu_custom_call" | custom-call | tf_op jit(solution)/shard_map/finish/pallas_call | solution.py:623
  106.4 0.0 copy-start
  106.4 1.6 %copy.16 = bf16[128,512]{1,0:T(8,128)(2,1)} copy(bf16[128,512]{1,0:T(8,128)(2,1)} %get-tuple-element.30) | data formatting | bytes 262144
  108.1 2.1 %copy.17 = bf16[1,96,32,128]{3,2,1,0:T(8,128)(2,1)} copy(bf16[1,96,32,128]{3,2,1,0:T(8,128)(2,1)} %get-tuple-element.31) | data formatting | bytes 1572864
  110.1 2.1 %copy.18 = bf16[1,96,32,128]{3,2,1,0:T(8,128)(2,1)} copy(bf16[1,96,32,128]{3,2,1,0:T(8,128)(2,1)} %get-tuple-element.32) | data formatting | bytes 1572864
  112.2 0.0 copy-done
  112.2 0.9 copy.19
  (5 shorter events, 0.0 us)
Async XLA Ops:
  106.4 5.8 %copy-start = (bf16[1,96,32,128]{3,2,1,0:T(8,128)(2,1)S(1)}, bf16[1,96,32,128]{3,2,1,0:T(8,128)(2,1)}, u32[]{:S(2)}) copy-start(bf16[1,96,32,128]{3,2,1,0:T(8,128)(2,1)} %get-tuple-element.33) | copy-start | bytes 2359300

commit v3 on v2

--- a/solution.py
+++ b/solution.py
@@ -568,7 +568,7 @@
                     per, rows, BLOCK
                 )
 
-    def keep_live(i, out, by_feat):
+    def pick_blocks(i, out, by_feat):
         @pl.loop(0, slots // SLOT_UNROLL)
         def _(n):
             for u in range(SLOT_UNROLL):
@@ -577,20 +577,19 @@
                 c = jnp.maximum(e, 0)
                 d, h = c // hidden_rows, c % hidden_rows
                 at = d * hidden_rows + h if by_feat else h * feat_blocks + d
-                block = dense[at]
-                out[0, k] = jnp.where(e >= 0, block, jnp.zeros_like(block))
+                out[0, k] = dense[at]
 
     load_gg.wait()
     load_xt.wait()
     all_products(xt, gg, hidden_rows)
-    keep_live(0, ggw_ref, False)
+    pick_blocks(0, ggw_ref, False)
     load_gu.wait()
     all_products(xt, gu, hidden_rows)
-    keep_live(1, guw_ref, False)
+    pick_blocks(1, guw_ref, False)
     load_ht.wait()
     load_cot.wait()
     all_products(ht, cot, feat_blocks)
-    keep_live(2, gdw_ref, True)
+    pick_blocks(2, gdw_ref, True)
 
     for step in range(1, span):
         at = (z + step) % span
@@ -655,7 +654,9 @@
     part, gg, gu, xt, ht = layer(
         both, gate_w, up_w, down_w, lists, tables, counts, hidden_rows, groups, tensor_size // 2
     )
-    return finish(part, gg, gu, xt, ht, both, lists, tensor_size, groups)
+    grad_x, *grads = finish(part, gg, gu, xt, ht, both, lists, tensor_size, groups)
+    live = (lists >= 0)[:, None, :, None, None]
+    return grad_x, *(jnp.where(live[i], grad, jnp.zeros_like(grad)) for i, grad in enumerate(grads))
 
 
 def fits(mesh):

time: 114 us -> 111 us (0.974); the launches traced: 113 us -> 111 us
  local copies, waits for them, and re-layouts: 6.65 us -> 0.67 us
  other arithmetic: 3.43 us -> 7.33 us
    unnamed x6 -> x5, local copies, waits for them, and re-layouts: 6.65 us -> 0.66 us
    select_n x0 -> x2, other arithmetic: none -> 3.91 us  [on_device(): jnp.where(live[i], grad, jnp.zeros_like(grad))]
    pallas_call x1, Pallas kernels: 31.1 us -> 32.2 us  [finish(): pl.pallas_call(functools.partial(finish_kernel, hidden_rows, feat_blocks,...]
where the time goes in v3:
time: 111 us
  Pallas kernels  103 us (93%)
  other arithmetic  7.33 us (7%)
    pallas_call x1, Pallas kernels, gather(): pl.pallas_call(functools.partial(gather_kernel, span), out_shape=jax.Shap...  44.5 us
    pallas_call x1, Pallas kernels, finish(): pl.pallas_call(functools.partial(finish_kernel, hidden_rows, feat_blocks,...  32.2 us
    pallas_call x1, Pallas kernels, layer(): pl.pallas_call(functools.partial(layer_kernel, hidden_rows, feat_blocks,...  25.9 us
    select_n x2, other arithmetic, on_device(): jnp.where(live[i], grad, jnp.zeros_like(grad))  3.91 us

profile of v3, /device:TPU:0, one launch (start us, length us, event | category | flops | bytes accessed | tf_op | source)
XLA Modules:
  0.0 111.4 jit_solution(15657786033399328025)
XLA Ops:
  0.6 1.4 %add_select_fusion = (s32[3,96]{1,0:T(4,128)S(1)}, s32[3,96]{1,0:T(4,128)S(1)}, s32[3]{0:T(128)S(1)}, pred[3,96]{1,0:T(4,128)(4,1)S(1)}, s32[3,96]{1,0:T(4,128)}) fusion(s32[1,96]{1,0:T(1,128)} %param.15, s32[1,96]{1,0:T(1,128)} %param.14, s32[1,96]{1,0:T(1,128)} %param.13), kind=kLoop, calls=%fused_computation.15 | loop fusion | flops 5181 | bytes 4908 | tf_op jit(solution)/shard_map/jit(floor_divide)/jit(_where)/select_n | solution.py:129
  2.0 0.1 convert_reduce_fusion.1
  2.2 0.1 fusion.5
  2.3 0.1 select_reduce_fusion.3
  2.4 0.2 convert_reduce_fusion
  2.7 0.2 select_reduce_fusion.2
  2.9 0.6 pad_add_fusion.tables
  3.5 0.6 pad_add_fusion.2.counts
  4.1 44.5 %gather.1.both_hbm = bf16[2,32,512,128]{3,2,1,0:T(8,128)(2,1)} custom-call(bf16[128,512]{1,0:T(8,128)(2,1)} %x_ref.1, bf16[128,512]{1,0:T(8,128)(2,1)} %cot_ref.1), custom_call_target="tpu_custom_call" | custom-call | tf_op jit(solution)/shard_map/gather/pallas_call | solution.py:486
  48.6 25.9 %layer.1 = (bf16[2,4,4,128,128]{4,3,2,1,0:T(8,128)(2,1)}, bf16[16,512,128]{2,1,0:T(8,128)(2,1)}, bf16[16,512,128]{2,1,0:T(8,128)(2,1)}, bf16[1024,512]{1,0:T(8,128)(2,1)}, bf16[512,512]{1,0:T(8,128)(2,1)}) custom-call(s32[6]{0:T(128)} %pad_add_fusion.2.counts, s32[9,112]{1,0:T(8,128)} %pad_add_fusion.tables, s32[3,96]{1,0:T(4,128)} %get-tuple-element.33.lists, ...), custom_call_target="tpu_custom_call" | custom-call | tf_op jit(solution)/shard_map/layer/pallas_call | solution.py:295
  74.5 32.2 %finish.1 = (bf16[128,512]{1,0:T(8,128)(2,1)}, bf16[1,96,32,128]{3,2,1,0:T(8,128)(2,1)}, bf16[1,96,32,128]{3,2,1,0:T(8,128)(2,1)}, bf16[1,96,32,128]{3,2,1,0:T(8,128)(2,1)}) custom-call(s32[3,96]{1,0:T(4,128)} %get-tuple-element.33.lists, bf16[2,4,4,128,128]{4,3,2,1,0:T(8,128)(2,1)} %get-tuple-element.13.part, ...), custom_call_target="tpu_custom_call" | custom-call | tf_op jit(solution)/shard_map/finish/pallas_call | solution.py:622
  106.8 0.0 copy-start
  106.8 0.0 copy-start.1
  106.8 2.9 %broadcast_select_fusion = (bf16[1,96,32,128]{3,2,1,0:T(8,128)(2,1)}, bf16[1,96,32,128]{3,2,1,0:T(8,128)(2,1)}) fusion(bf16[1,96,32,128]{3,2,1,0:T(8,128)(2,1)} %get-tuple-element.21, pred[96]{0:T(512)(128)(4,1)S(1)} %get-tuple-element.34, bf16[1,96,32,128]{3,2,1,0:T(8,128)(2,1)} %get-tuple-element.20, pred[96]{0:T(512)(128)(4,1)S(1)} %get-tuple-element.35), kind=kLoop, calls=%fused_computation | loop fusion | flops 786432 | bytes 3145920 | tf_op jit(solution)/shard_map/jit(_where)/select_n | solution.py:659
  109.7 0.0 copy-done
  109.7 1.1 broadcast_select_fusion.2
  110.7 0.0 copy-done.1
  110.7 0.7 copy.13
  (6 shorter events, 0.0 us)
Async XLA Ops:
  106.8 2.9 %copy-start = (bf16[1,96,32,128]{3,2,1,0:T(8,128)(2,1)S(1)}, bf16[1,96,32,128]{3,2,1,0:T(8,128)(2,1)}, u32[]{:S(2)}) copy-start(bf16[1,96,32,128]{3,2,1,0:T(8,128)(2,1)} %get-tuple-element.19) | copy-start | bytes 2359300
  106.8 3.9 %copy-start.1 = (bf16[128,512]{1,0:T(8,128)(2,1)S(1)}, bf16[128,512]{1,0:T(8,128)(2,1)}, u32[]{:S(2)}) copy-start(bf16[128,512]{1,0:T(8,128)(2,1)} %get-tuple-element.43) | copy-start | bytes 393220
